TPU v7x, 32 devices: a whole 2x2x4 slice. The times are simulated.
32 devices in a mesh: outer: 4 (over x, core), dp: 2 (over y), mp: 4 (over z).
Axes of the slice: x: 2, y: 2, z: 4, core: 2. Of those that a mesh axis runs over, the one named last changes fastest.
Arguments:
- inputs: bfloat16 [384, 4096], P('outer', 'dp'), may hold values from -6 to 6
- out_grad: bfloat16 [384, 4096], P('outer', 'dp'), may hold values from -0.59765625 to 0.59765625
- w_gate: bfloat16 [4096, 12288], P('dp', 'mp'), may hold values from -0.09375 to 0.09375
- w_up: bfloat16 [4096, 12288], P('dp', 'mp'), may hold values from -0.09375 to 0.09375
- w_down: bfloat16 [12288, 4096], P('mp', 'dp'), may hold values from -0.0546875 to 0.0546875
Outputs:
- input_grad: bfloat16 [384, 4096], P('outer', 'dp')
- gate_grad: bfloat16 [4096, 12288], P('dp', 'mp')
- up_grad: bfloat16 [4096, 12288], P('dp', 'mp')
- down_grad: bfloat16 [12288, 4096], P('mp', 'dp')
All inputs are finite; a program needn't handle non-finite values.
Results may differ from a plain program's by a relative error of at most 0.017.
Values may be sent and summed in bfloat16 or wider, within the bound.
A program may use at most 256 MiB of HBM per device.

v0:
```python
import jax
import jax.numpy as jnp
from jax import lax
from jax.sharding import PartitionSpec as P


def transposed_left(left, right):
    return lax.dot_general(
        left, right, (((0,), (0,)), ((), ())), preferred_element_type=jnp.float32
    )


def transposed_right(left, right):
    return lax.dot_general(
        left, right, (((1,), (1,)), ((), ())), preferred_element_type=jnp.float32
    )


def on_device(inputs, out_grad, w_gate, w_up, w_down):
    hidden_cols = w_gate.shape[1]
    rows_in = inputs
    summed = lax.psum_scatter(
        jnp.concatenate(
            [
                jnp.dot(rows_in, w_gate, preferred_element_type=jnp.float32),
                jnp.dot(rows_in, w_up, preferred_element_type=jnp.float32),
            ],
            axis=1,
        ).astype(jnp.bfloat16),
        "dp",
        scatter_dimension=0,
        tiled=True,
    ).astype(jnp.float32)
    gate = summed[:, :hidden_cols]
    up = summed[:, hidden_cols:]
    rows_grad = out_grad
    hidden_grad = lax.psum_scatter(
        transposed_right(rows_grad, w_down).astype(jnp.bfloat16),
        "dp",
        scatter_dimension=0,
        tiled=True,
    ).astype(jnp.float32)
    sig = jax.nn.sigmoid(gate)
    hidden = (gate * sig * up).astype(jnp.bfloat16)
    gate_term = (hidden_grad * up * sig * (1.0 + gate * (1.0 - sig))).astype(jnp.bfloat16)
    up_term = (hidden_grad * gate * sig).astype(jnp.bfloat16)
    piece_hidden = lax.all_gather(hidden, "dp", axis=0, tiled=True)
    piece_gate = lax.all_gather(gate_term, "dp", axis=0, tiled=True)
    piece_up = lax.all_gather(up_term, "dp", axis=0, tiled=True)
    rows_in = inputs
    rows_grad = out_grad
    down_acc = transposed_left(piece_hidden, rows_grad)
    gate_acc = transposed_left(rows_in, piece_gate)
    up_acc = transposed_left(rows_in, piece_up)
    rows_back = transposed_right(piece_gate, w_gate) + transposed_right(piece_up, w_up)
    input_grad = lax.psum(rows_back.astype(jnp.bfloat16), "mp")
    down_sum, gate_sum, up_sum = (
        lax.psum(down_acc.astype(jnp.bfloat16), "outer").astype(jnp.float32),
        lax.psum(gate_acc.astype(jnp.bfloat16), "outer").astype(jnp.float32),
        lax.psum(up_acc.astype(jnp.bfloat16), "outer").astype(jnp.float32),
    )
    return (
        input_grad,
        gate_sum.astype(jnp.bfloat16),
        up_sum.astype(jnp.bfloat16),
        down_sum.astype(jnp.bfloat16),
    )


def solution(mesh):
    in_specs = (P("outer", "dp"), P("outer", "dp"), P("dp", "mp"), P("dp", "mp"), P("mp", "dp"))
    out_specs = (P("outer", "dp"), P("dp", "mp"), P("dp", "mp"), P("mp", "dp"))
    return jax.shard_map(
        on_device, mesh=mesh, in_specs=in_specs, out_specs=out_specs, check_vma=False
    )
```

profile of v0, /device:TPU:0, one launch (start us, length us, event | category | flops | bytes accessed | tf_op | source)
XLA Modules:
  0.0 796.7 jit_solution(5428519828147046687)
XLA Ops:
  7.2 0.0 copy-start
  7.2 0.0 reduce-scatter.5.cloned.1.call-start
  7.2 0.9 copy-done
  8.2 0.0 copy-start.2
  8.2 6.8 convolution_convert_fusion.2
  15.0 1.3 copy-done.2
  16.3 0.0 copy-start.3
  16.3 2.1 convolution_convert_fusion.1
  18.4 1.1 pad_maximum_fusion
  19.5 0.0 reduce-scatter.5.cloned.1.call-update
  19.6 0.0 reduce-scatter.3.cloned.1.call-start
  19.6 0.0 copy-done.3
  19.6 9.4 %convolution_convert_fusion.3 = bf16[96,3072]{1,0:T(8,128)(2,1)} fusion(bf16[96,2048]{1,0:T(8,128)(2,1)S(1)} %copy-done.3, bf16[3072,2048]{1,0:T(8,128)(2,1)} %param.9), kind=kOutput, calls=%fused_computation.5 | convolution fusion | flops 1208254464 | bytes 13565952 | tf_op jit(solution)/shard_map/dot_general | solution.py:14
  29.0 0.0 reduce-scatter.3.cloned.1.call-update
  29.0 0.0 all-reduce.6.cloned.1.call-start
  29.1 15.1 %reduce-scatter.5.cloned.1.call-done = bf16[48,6144]{1,0:T(8,128)(2,1)} async-done(((bf16[96,6144]{1,0:T(8,128)(2,1)}), bf16[48,6144]{1,0:T(8,128)(2,1)}) %reduce-scatter.5.cloned.1.call-update) | async-done | bytes 589840 | tf_op jit(solution)/shard_map/reduce_scatter | solution.py:22
  44.2 1.1 convert_element_type.45
  45.3 17.1 %reduce-scatter.3.cloned.1.call-done = bf16[48,3072]{1,0:T(8,128)(2,1)} async-done(((bf16[96,3072]{1,0:T(8,128)(2,1)}), bf16[48,3072]{1,0:T(8,128)(2,1)}) %reduce-scatter.3.cloned.1.call-update) | async-done | bytes 294928 | tf_op jit(solution)/shard_map/reduce_scatter | solution.py:37
  62.4 1.3 fusion.5
  63.7 9.4 %all_gather.10 = bf16[96,3072]{1,0:T(8,128)(2,1)S(1)} all-gather(bf16[48,3072]{1,0:T(8,128)(2,1)S(1)} %get-tuple-element.11), channel_id=1, replica_groups=mesh['outer'=4,'dp'=2,'mp'=4] {'dp'}, dimensions={0}, use_global_device_ids=true | all-gather | bytes 884736 | tf_op jit(solution)/shard_map/all_gather | solution.py:49
  73.1 8.5 %all_gather.9 = bf16[96,3072]{1,0:T(8,128)(2,1)S(1)} all-gather(bf16[48,3072]{1,0:T(8,128)(2,1)S(1)} %get-tuple-element.12), channel_id=1, replica_groups=mesh['outer'=4,'dp'=2,'mp'=4] {'dp'}, dimensions={0}, use_global_device_ids=true | all-gather | bytes 884736 | tf_op jit(solution)/shard_map/all_gather | solution.py:48
  81.7 7.8 all_gather.11
  89.5 6.6 convert_bitcast_fusion
  96.1 6.6 convert_bitcast_fusion.1
  102.7 6.6 convolution_convert_fusion
  109.3 0.0 all-reduce.6.cloned.1.call-update
  109.3 0.0 all-reduce.4.cloned.1.call-start
  109.4 8.5 %fusion.6 = f32[96,2048]{1,0:T(8,128)S(1)} fusion(bf16[96,3072]{1,0:T(8,128)(2,1)S(1)} %all_gather.9, bf16[2048,3072]{1,0:T(8,128)(2,1)} %param.7), kind=kOutput, calls=%fused_computation.18 | convolution fusion | flops 1207959552 | bytes 13959168 | tf_op jit(solution)/shard_map/dot_general | solution.py:14
  117.9 9.3 %fusion = bf16[96,2048]{1,0:T(8,128)(2,1)} fusion(f32[96,2048]{1,0:T(8,128)S(1)} %fusion.6, bf16[96,3072]{1,0:T(8,128)(2,1)S(1)} %all_gather.10, bf16[2048,3072]{1,0:T(8,128)(2,1)} %param.8), kind=kOutput, calls=%fused_computation.7 | convolution fusion | flops 1208352768 | bytes 14352384 | tf_op jit(solution)/shard_map/dot_general | solution.py:14
  127.2 0.0 all-reduce.4.cloned.1.call-update
  127.3 610.4 %all-reduce.6.cloned.1.call-done = (bf16[2048,3072]{0,1:T(8,128)(2,1)}, bf16[2048,3072]{0,1:T(8,128)(2,1)}, bf16[3072,2048]{1,0:T(8,128)(2,1)}) async-done(((bf16[2048,3072]{0,1:T(8,128)(2,1)}, bf16[2048,3072]{0,1:T(8,128)(2,1)}, bf16[3072,2048]{1,0:T(8,128)(2,1)}), (bf16[2048,3072]{0,1:T(8,128)(2,1)}, bf16[2048,3072]{0,1:T(8,128)(2,1)}, bf16[3072,2048]{1,0:T(8,128)(2,1)})) %all-reduce.6.cloned.1.call-update) | async-done | bytes 37748752 | tf_op jit(solution)/shard_map/psum | solution.py:59
  737.6 16.6 %copy.9 = bf16[2048,3072]{1,0:T(8,128)(2,1)} copy(bf16[2048,3072]{0,1:T(8,128)(2,1)} %get-tuple-element.8) | data formatting | bytes 25165824
  754.2 16.6 %copy.10 = bf16[2048,3072]{1,0:T(8,128)(2,1)} copy(bf16[2048,3072]{0,1:T(8,128)(2,1)} %get-tuple-element.9) | data formatting | bytes 25165824
  770.8 6.8 all-reduce.4.cloned.1.call-done
  777.6 0.0 copy-start.1
  777.6 1.8 copy.15
  779.4 10.7 %copy.16 = bf16[3072,2048]{1,0:T(8,128)(2,1)} copy(bf16[3072,2048]{1,0:T(8,128)(2,1)} %get-tuple-element.17) | data formatting | bytes 25165824
  790.2 0.0 copy-done.1
Async XLA Ops:
  7.2 1.0 copy-start
  7.2 37.0 %reduce-scatter.5.cloned.1.call-start = ((), (), s32[]{:S(2)}) async-start(), calls=%async_computation.3 | async-start | bytes 1769472 | tf_op jit(solution)/shard_map/reduce_scatter | solution.py:22
  8.2 8.2 %copy-start.2 = (bf16[2048,3072]{1,0:T(8,128)(2,1)S(1)}, bf16[2048,3072]{1,0:T(8,128)(2,1)}, u32[]{:S(2)}) copy-start(bf16[2048,3072]{1,0:T(8,128)(2,1)} %param.8) | copy-start | bytes 37748740
  16.3 3.3 copy-start.3
  19.6 42.9 %reduce-scatter.3.cloned.1.call-start = ((), (), s32[]{:S(2)}) async-start(), calls=%async_computation.2 | async-start | bytes 884736 | tf_op jit(solution)/shard_map/reduce_scatter | solution.py:37
  29.0 708.6 %all-reduce.6.cloned.1.call-start = ((), (), s32[]{:S(2)}) async-start(), calls=%async_computation.5 | async-start | bytes 75497472 | tf_op jit(solution)/shard_map/psum | solution.py:59
  109.3 668.3 %all-reduce.4.cloned.1.call-start = ((), (), s32[]{:S(2)}) async-start(), calls=%async_computation.4 | async-start | bytes 786432 | tf_op jit(solution)/shard_map/psum | solution.py:56
  777.6 12.5 %copy-start.1 = (bf16[96,2048]{1,0:T(8,128)(2,1)S(1)}, bf16[96,2048]{1,0:T(8,128)(2,1)}, u32[]{:S(2)}) copy-start(bf16[96,2048]{1,0:T(8,128)(2,1)} %param.5) | copy-start | bytes 1179652
Sparse Core Ops, SparseCore 0:
  19.7 24.4 reduce-scatter.4
  47.1 15.2 reduce-scatter.2
  109.4 628.1 all-reduce.5
  740.5 37.0 all-reduce.3
where the time goes:
time: 798 us; the launch traced here: 797 us
  waiting for transfers between devices  649 us (81%)
  matrix products  56 us (7%)
  local copies, waits for them, and re-layouts  48 us (6%)
  blocking collectives  25.8 us (3%)
  between operations  13.8 us (2%)
    psum x1, waiting for transfers between devices, on_device(): lax.psum(gate_acc.astype(jnp.bfloat16), 'outer').astype(jnp.float32)  610 us
    unnamed x12, local copies, waits for them, and re-layouts  48 us
    dot_general x3, matrix products, transposed_right(): lax.dot_general(left, right, (((1,), (1,)), ((), ())), preferred_element_...  27.2 us
    dot_general x3, matrix products, transposed_left(): lax.dot_general(left, right, (((0,), (0,)), ((), ())), preferred_element_...  19.8 us
    reduce_scatter x1, waiting for transfers between devices, on_device(): lax.psum_scatter(transposed_right(rows_grad, w_down).astype(jnp.bfloat16)...  17.1 us
  transfers between devices with their start and end apart: 4, of which 4 were waited for; matrix products, arithmetic and copies ran while one was open for 8% of the time, Pallas kernels for 0%

commit v1 on v0

v1 whole, which is shorter than its diff:
```python
import jax
import jax.numpy as jnp
from jax import lax
from jax.sharding import PartitionSpec as P

BF16 = jnp.bfloat16


def mm(left, right, dims):
    return lax.dot_general(left, right, (dims, ((), ())), preferred_element_type=jnp.float32)


def transposed_left(left, right):
    return mm(left, right, ((0,), (0,)))


def transposed_right(left, right):
    return mm(left, right, ((1,), (1,)))


def terms_of(gate, up, hidden_grad):
    sig = jax.nn.sigmoid(gate)
    hidden = (gate * sig * up).astype(BF16)
    gate_term = (hidden_grad * up * sig * (1.0 + gate * (1.0 - sig))).astype(BF16)
    up_term = (hidden_grad * gate * sig).astype(BF16)
    return hidden, gate_term, up_term


def summed_over_dp(partial, dp):
    if dp == 2:
        other = lax.ppermute(partial, "dp", [(0, 1), (1, 0)])
        return partial.astype(jnp.float32) + other.astype(jnp.float32)
    part = lax.psum_scatter(partial, "dp", scatter_dimension=0, tiled=True)
    return lax.all_gather(part, "dp", axis=0, tiled=True).astype(jnp.float32)


def on_device(dp, inputs, out_grad, w_gate, w_up, w_down):
    all_in = lax.all_gather(inputs, "outer", axis=0, tiled=True)
    all_grad = lax.all_gather(out_grad, "outer", axis=0, tiled=True)
    gate = summed_over_dp(mm(inputs, w_gate, ((1,), (0,))).astype(BF16), dp)
    up = summed_over_dp(mm(inputs, w_up, ((1,), (0,))).astype(BF16), dp)
    hidden_grad = summed_over_dp(transposed_right(out_grad, w_down).astype(BF16), dp)
    hidden, gate_term, up_term = terms_of(gate, up, hidden_grad)
    all_hidden = lax.all_gather(hidden, "outer", axis=0, tiled=True)
    all_up = lax.all_gather(up_term, "outer", axis=0, tiled=True)
    all_gate = lax.all_gather(gate_term, "outer", axis=0, tiled=True)
    rows_back = transposed_right(gate_term, w_gate) + transposed_right(up_term, w_up)
    input_grad = lax.psum(rows_back.astype(BF16), "mp")
    down_grad = transposed_left(all_hidden, all_grad).astype(BF16)
    up_grad = transposed_left(all_in, all_up).astype(BF16)
    gate_grad = transposed_left(all_in, all_gate).astype(BF16)
    return input_grad, gate_grad, up_grad, down_grad


def solution(mesh):
    dp = mesh.shape["dp"]
    in_specs = (P("outer", "dp"), P("outer", "dp"), P("dp", "mp"), P("dp", "mp"), P("mp", "dp"))
    out_specs = (P("outer", "dp"), P("dp", "mp"), P("dp", "mp"), P("mp", "dp"))

    def body(*arrays):
        return on_device(dp, *arrays)

    return jax.shard_map(body, mesh=mesh, in_specs=in_specs, out_specs=out_specs, check_vma=False)
```

time: 798 us -> 214 us (0.27)
  waiting for transfers between devices: 649 us -> 85.7 us
  blocking collectives: 25.8 us -> 0 us
  matrix products: 56 us -> 69.7 us
  local copies, waits for them, and re-layouts: 48 us -> 36.5 us
    psum x2 -> x1, waiting for transfers between devices: 617 us -> 0.01 us  [on_device(): input_grad = lax.psum(rows_back.astype(BF16), 'mp')]
    all_gather x0 -> x5, waiting for transfers between devices: none -> 56.6 us  [the longest x1 26.2 us: on_device(): all_hidden = lax.all_gather(hidden, 'outer', axis=0, tiled=True)]
    reduce_scatter x2 -> x0, waiting for transfers between devices: 32.2 us -> none  [the longest x1 17.1 us: on_device(): lax.psum_scatter(transposed_right(rows_grad, w_down).astype(jnp.bfloat16)...]
    ppermute x0 -> x3, waiting for transfers between devices: none -> 27.4 us  [summed_over_dp(): other = lax.ppermute(partial, 'dp', [(0, 1), (1, 0)])]
    all_gather x3 -> x0, blocking collectives: 25.8 us -> none  [the longest x1 9.42 us: on_device(): piece_up = lax.all_gather(up_term, 'dp', axis=0, tiled=True)]
    dot_general x8, matrix products: 56 us -> 69.7 us  [mm(): lax.dot_general(left, right, (dims, ((), ())), preferred_element_type=jnp...]
    unnamed x12 -> x13, local copies, waits for them, and re-layouts: 48 us -> 36.5 us
  transfers between devices with their start and end apart: 4 -> 9, of which waited for: 4 -> 7; matrix products, arithmetic and copies ran while one was open for 8% -> 45% of each run, Pallas kernels for 0% -> 0%
where the time goes in v1:
time: 214 us; the launch traced here: 213 us
  waiting for transfers between devices  85.7 us (40%)
  matrix products  69.7 us (33%)
  local copies, waits for them, and re-layouts  36.5 us (17%)
  between operations  15.3 us (7%)
  starting transfers between devices  4.1 us (2%)
    dot_general x8, matrix products, mm(): lax.dot_general(left, right, (dims, ((), ())), preferred_element_type=jnp...  69.7 us
    unnamed x13, local copies, waits for them, and re-layouts  36.5 us
    ppermute x3, waiting for transfers between devices, summed_over_dp(): other = lax.ppermute(partial, 'dp', [(0, 1), (1, 0)])  27.4 us
    all_gather x1, waiting for transfers between devices, on_device(): all_hidden = lax.all_gather(hidden, 'outer', axis=0, tiled=True)  26.2 us
    all_gather x1, waiting for transfers between devices, on_device(): all_gate = lax.all_gather(gate_term, 'outer', axis=0, tiled=True)  14.9 us
    all_gather x1, waiting for transfers between devices, on_device(): all_grad = lax.all_gather(out_grad, 'outer', axis=0, tiled=True)  9.91 us
    all_gather x1, waiting for transfers between devices, on_device(): all_up = lax.all_gather(up_term, 'outer', axis=0, tiled=True)  5.57 us
  transfers between devices with their start and end apart: 9, of which 7 were waited for; matrix products, arithmetic and copies ran while one was open for 45% of the time, Pallas kernels for 0%

profile of v1, /device:TPU:0, one launch (start us, length us, event | category | flops | bytes accessed | tf_op | source)
XLA Modules:
  0.0 213.4 jit_solution(7821339926576694047)
XLA Ops:
  8.0 0.0 copy-start.1
  8.0 0.0 all-gather.8.cloned.1.call-start
  8.1 8.7 %convolution_convert_fusion.3 = bf16[96,3072]{1,0:T(8,128)(2,1)S(1)} fusion(bf16[96,2048]{1,0:T(8,128)(2,1)} %param.6, bf16[3072,2048]{1,0:T(8,128)(2,1)} %param.9), kind=kOutput, calls=%fused_computation.5 | convolution fusion | flops 1208254464 | bytes 13565952 | tf_op jit(solution)/shard_map/dot_general | solution.py:10
  16.8 3.0 %collective-permute-start = (bf16[96,3072]{1,0:T(8,128)(2,1)S(1)}, bf16[96,3072]{1,0:T(8,128)(2,1)S(1)}, u32[]{:S(2)}, u32[]{:S(2)}) collective-permute-start(bf16[96,3072]{1,0:T(8,128)(2,1)S(1)} %convolution_convert_fusion.3), channel_id=1, source_target_pairs={{0,4},{4,0},{1,5},{5,1},{2,6},{6,2},{3,7},{7,3},{8,12},{12,8},{9,1... | collective-permute-start | bytes 1769480 | tf_op jit(solution)/shard_map/ppermute | solution.py:31
  19.8 0.0 all-gather.8.cloned.1.call-update
  19.8 0.0 all-gather.10.cloned.1.call-start
  19.9 0.0 copy-done.1
  19.9 0.0 copy-start
  19.9 6.8 %convolution_convert_fusion.2 = bf16[96,3072]{1,0:T(8,128)(2,1)S(1)} fusion(bf16[96,2048]{1,0:T(8,128)(2,1)S(1)} %copy-done.1, bf16[2048,3072]{1,0:T(8,128)(2,1)} %param.8), kind=kOutput, calls=%fused_computation.4 | convolution fusion | flops 1208254464 | bytes 13565952 | tf_op jit(solution)/shard_map/dot_general | solution.py:10
  26.8 0.1 collective-permute-start.1
  26.8 1.5 copy-done
  28.3 2.1 convolution_convert_fusion.1
  30.5 0.6 collective-permute-start.2
  31.0 3.0 %collective-permute-done = bf16[96,3072]{1,0:T(8,128)(2,1)S(1)} collective-permute-done((bf16[96,3072]{1,0:T(8,128)(2,1)S(1)}, bf16[96,3072]{1,0:T(8,128)(2,1)S(1)}, u32[]{:S(2)}, u32[]{:S(2)}) %collective-permute-start) | collective-permute-done | bytes 589856 | tf_op jit(solution)/shard_map/ppermute | solution.py:31
  34.0 12.6 %collective-permute-done.1 = bf16[96,3072]{1,0:T(8,128)(2,1)S(1)} collective-permute-done((bf16[96,3072]{1,0:T(8,128)(2,1)S(1)}, bf16[96,3072]{1,0:T(8,128)(2,1)S(1)}, u32[]{:S(2)}, u32[]{:S(2)}) %collective-permute-start.1) | collective-permute-done | bytes 589856 | tf_op jit(solution)/shard_map/ppermute | solution.py:31
  46.6 11.8 %collective-permute-done.2 = bf16[96,3072]{1,0:T(8,128)(2,1)S(1)} collective-permute-done((bf16[96,3072]{1,0:T(8,128)(2,1)S(1)}, bf16[96,3072]{1,0:T(8,128)(2,1)S(1)}, u32[]{:S(2)}, u32[]{:S(2)}) %collective-permute-start.2) | collective-permute-done | bytes 589856 | tf_op jit(solution)/shard_map/ppermute | solution.py:31
  58.4 2.1 multiply_convert_fusion
  60.5 0.0 copy-start.3
  60.5 0.0 all-gather.10.cloned.1.call-update
  60.5 0.0 all-gather.6.cloned.1.call-start
  60.6 0.7 all-gather.6.cloned.1.call-update
  61.3 0.0 all-gather.14.cloned.1.call-start
  61.3 0.5 all-gather.14.cloned.1.call-update
  61.8 0.0 all-gather.12.cloned.1.call-start
  61.9 0.5 all-gather.12.cloned.1.call-update
  62.4 0.0 copy-start.2
  62.4 0.2 all-reduce.2.cloned.1.call-start
  62.7 0.0 copy-done.3
  62.7 8.6 %fusion.1 = f32[96,2048]{1,0:T(8,128)S(1)} fusion(bf16[96,3072]{1,0:T(8,128)(2,1)S(1)} %copy-done.3, bf16[2048,3072]{1,0:T(8,128)(2,1)} %param.7), kind=kOutput, calls=%fused_computation.15 | convolution fusion | flops 1207959552 | bytes 13959168 | tf_op jit(solution)/shard_map/dot_general | solution.py:10
  71.2 0.0 copy-done.2
  71.2 9.3 %fusion = bf16[96,2048]{1,0:T(8,128)(2,1)} fusion(f32[96,2048]{1,0:T(8,128)S(1)} %fusion.1, bf16[96,3072]{1,0:T(8,128)(2,1)S(1)} %copy-done.2, bf16[2048,3072]{1,0:T(8,128)(2,1)} %param.8), kind=kOutput, calls=%fused_computation.7 | convolution fusion | flops 1208352768 | bytes 14352384 | tf_op jit(solution)/shard_map/dot_general | solution.py:10
  80.6 0.0 all-reduce.2.cloned.1.call-update
  80.6 0.0 all-gather.8.cloned.1.call-done
  80.6 0.0 copy-start.4
  80.6 5.6 %all-gather.10.cloned.1.call-done = bf16[384,3072]{1,0:T(8,128)(2,1)} async-done(((bf16[96,3072]{1,0:T(8,128)(2,1)}), bf16[384,3072]{1,0:T(8,128)(2,1)}) %all-gather.10.cloned.1.call-update) | async-done | bytes 2359312 | tf_op jit(solution)/shard_map/all_gather | solution.py:45
  86.2 11.5 %convert_bitcast_fusion = bf16[2048,3072]{0,1:T(8,128)(2,1)} fusion(bf16[384,3072]{1,0:T(8,128)(2,1)} %all-gather.10.cloned.1.call-done, bf16[384,2048]{1,0:T(8,128)(2,1)} %all-gather.8.cloned.1.call-done), kind=kOutput, calls=%fused_computation | convolution fusion | flops 4838129664 | bytes 16515072 | tf_op jit(solution)/shard_map/dot_general | solution.py:10
  97.7 14.9 %all-gather.6.cloned.1.call-done = bf16[384,3072]{1,0:T(8,128)(2,1)} async-done(((bf16[96,3072]{1,0:T(8,128)(2,1)}), bf16[384,3072]{1,0:T(8,128)(2,1)}) %all-gather.6.cloned.1.call-update) | async-done | bytes 2359312 | tf_op jit(solution)/shard_map/all_gather | solution.py:46
  112.6 0.0 copy-done.4
  112.6 11.3 %convert_bitcast_fusion.1 = bf16[2048,3072]{0,1:T(8,128)(2,1)} fusion(bf16[384,3072]{1,0:T(8,128)(2,1)} %all-gather.6.cloned.1.call-done, bf16[384,2048]{1,0:T(8,128)(2,1)S(1)} %copy-done.4), kind=kOutput, calls=%fused_computation.1 | convolution fusion | flops 4838129664 | bytes 16515072 | tf_op jit(solution)/shard_map/dot_general | solution.py:10
  123.9 9.9 %all-gather.14.cloned.1.call-done = bf16[384,2048]{1,0:T(8,128)(2,1)} async-done(((bf16[96,2048]{1,0:T(8,128)(2,1)}), bf16[384,2048]{1,0:T(8,128)(2,1)}) %all-gather.14.cloned.1.call-update) | async-done | bytes 1572880 | tf_op jit(solution)/shard_map/all_gather | solution.py:39
  133.8 26.2 %all-gather.12.cloned.1.call-done = bf16[384,3072]{1,0:T(8,128)(2,1)} async-done(((bf16[96,3072]{1,0:T(8,128)(2,1)}), bf16[384,3072]{1,0:T(8,128)(2,1)}) %all-gather.12.cloned.1.call-update) | async-done | bytes 2359312 | tf_op jit(solution)/shard_map/all_gather | solution.py:44
  159.9 11.4 %convolution_convert_fusion = bf16[3072,2048]{1,0:T(8,128)(2,1)} fusion(bf16[384,3072]{1,0:T(8,128)(2,1)} %all-gather.12.cloned.1.call-done, bf16[384,2048]{1,0:T(8,128)(2,1)} %all-gather.14.cloned.1.call-done), kind=kOutput, calls=%fused_computation.2 | convolution fusion | flops 4838129664 | bytes 16515072 | tf_op jit(solution)/shard_map/dot_general | solution.py:10
  171.4 16.6 %copy.10 = bf16[2048,3072]{1,0:T(8,128)(2,1)} copy(bf16[2048,3072]{0,1:T(8,128)(2,1)} %convert_bitcast_fusion) | data formatting | bytes 25165824
  187.9 16.6 %copy.9 = bf16[2048,3072]{1,0:T(8,128)(2,1)} copy(bf16[2048,3072]{0,1:T(8,128)(2,1)} %convert_bitcast_fusion.1) | data formatting | bytes 25165824
  204.5 0.0 all-reduce.2.cloned.1.call-done
  204.5 1.8 copy.12
Async XLA Ops:
  8.0 11.9 %copy-start.1 = (bf16[96,2048]{1,0:T(8,128)(2,1)S(1)}, bf16[96,2048]{1,0:T(8,128)(2,1)}, u32[]{:S(2)}) copy-start(bf16[96,2048]{1,0:T(8,128)(2,1)} %param.5) | copy-start | bytes 1179652
  8.0 72.6 %all-gather.8.cloned.1.call-start = ((), (), s32[]{:S(2)}) async-start(), calls=%async_computation.2 | async-start | bytes 1966080 | tf_op jit(solution)/shard_map/all_gather | solution.py:38
  16.8 17.2 %collective-permute-start = (bf16[96,3072]{1,0:T(8,128)(2,1)S(1)}, bf16[96,3072]{1,0:T(8,128)(2,1)S(1)}, u32[]{:S(2)}, u32[]{:S(2)}) collective-permute-start(bf16[96,3072]{1,0:T(8,128)(2,1)S(1)} %convolution_convert_fusion.3), channel_id=1, source_target_pairs={{0,4},{4,0},{1,5},{5,1},{2,6},{6,2},{3,7},{7,3},{8,12},{12,8},{9,1... | collective-permute-start | bytes 1769480 | tf_op jit(solution)/shard_map/ppermute | solution.py:31
  19.8 66.4 %all-gather.10.cloned.1.call-start = ((), (), s32[]{:S(2)}) async-start(), calls=%async_computation.3 | async-start | bytes 2949120 | tf_op jit(solution)/shard_map/all_gather | solution.py:45
  19.9 8.4 %copy-start = (bf16[2048,3072]{1,0:T(8,128)(2,1)S(1)}, bf16[2048,3072]{1,0:T(8,128)(2,1)}, u32[]{:S(2)}) copy-start(bf16[2048,3072]{1,0:T(8,128)(2,1)} %param.7) | copy-start | bytes 37748740
  26.8 19.9 %collective-permute-start.1 = (bf16[96,3072]{1,0:T(8,128)(2,1)S(1)}, bf16[96,3072]{1,0:T(8,128)(2,1)S(1)}, u32[]{:S(2)}, u32[]{:S(2)}) collective-permute-start(bf16[96,3072]{1,0:T(8,128)(2,1)S(1)} %convolution_convert_fusion.2), channel_id=1, source_target_pairs={{0,4},{4,0},{1,5},{5,1},{2,6},{6,2},{3,7},{7,3},{8,12},{12,8},{9,1... | collective-permute-start | bytes 1769480 | tf_op jit(solution)/shard_map/ppermute | solution.py:31
  30.5 28.0 %collective-permute-start.2 = (bf16[96,3072]{1,0:T(8,128)(2,1)S(1)}, bf16[96,3072]{1,0:T(8,128)(2,1)S(1)}, u32[]{:S(2)}, u32[]{:S(2)}) collective-permute-start(bf16[96,3072]{1,0:T(8,128)(2,1)S(1)} %convolution_convert_fusion.1), channel_id=1, source_target_pairs={{0,4},{4,0},{1,5},{5,1},{2,6},{6,2},{3,7},{7,3},{8,12},{12,8},{9,1... | collective-permute-start | bytes 1769480 | tf_op jit(solution)/shard_map/ppermute | solution.py:31
  60.5 2.2 %copy-start.3 = (bf16[96,3072]{1,0:T(8,128)(2,1)S(1)}, bf16[96,3072]{1,0:T(8,128)(2,1)}, u32[]{:S(2)}) copy-start(bf16[96,3072]{1,0:T(8,128)(2,1)} %get-tuple-element.9) | copy-start | bytes 1769476
  60.5 52.1 %all-gather.6.cloned.1.call-start = ((), (), s32[]{:S(2)}) async-start(), calls=%async_computation.1 | async-start | bytes 2949120 | tf_op jit(solution)/shard_map/all_gather | solution.py:46
  61.3 72.5 %all-gather.14.cloned.1.call-start = ((), (), s32[]{:S(2)}) async-start(), calls=%async_computation.5 | async-start | bytes 1966080 | tf_op jit(solution)/shard_map/all_gather | solution.py:39
  61.8 98.1 %all-gather.12.cloned.1.call-start = ((), (), s32[]{:S(2)}) async-start(), calls=%async_computation.4 | async-start | bytes 2949120 | tf_op jit(solution)/shard_map/all_gather | solution.py:44
  62.4 8.8 %copy-start.2 = (bf16[96,3072]{1,0:T(8,128)(2,1)S(1)}, bf16[96,3072]{1,0:T(8,128)(2,1)}, u32[]{:S(2)}) copy-start(bf16[96,3072]{1,0:T(8,128)(2,1)} %get-tuple-element.10) | copy-start | bytes 1769476
  62.4 142.1 %all-reduce.2.cloned.1.call-start = ((), (), s32[]{:S(2)}) async-start(), calls=%async_computation | async-start | bytes 786432 | tf_op jit(solution)/shard_map/psum | solution.py:48
  80.6 32.0 %copy-start.4 = (bf16[384,2048]{1,0:T(8,128)(2,1)S(1)}, bf16[384,2048]{1,0:T(8,128)(2,1)}, u32[]{:S(2)}) copy-start(bf16[384,2048]{1,0:T(8,128)(2,1)} %all-gather.8.cloned.1.call-done) | copy-start | bytes 4718596
Sparse Core Ops, SparseCore 0:
  20.0 19.9 all-gather.7
  60.6 25.5 all-gather.9
  88.4 24.1 all-gather.5
  114.1 19.6 all-gather.13
  135.8 24.0 all-gather.11
Sparse Core Ops, SparseCore 1:
  80.7 38.1 all-reduce.1

commit v2 on v1

--- a/solution.py
+++ b/solution.py
@@ -1,6 +1,10 @@
+import functools
+
 import jax
 import jax.numpy as jnp
 from jax import lax
+from jax.experimental import pallas as pl
+from jax.experimental.pallas import tpu as pltpu
 from jax.sharding import PartitionSpec as P
 
 BF16 = jnp.bfloat16
@@ -52,12 +56,253 @@
     return input_grad, gate_grad, up_grad, down_grad
 
 
+MESH = pl.DeviceIdType.MESH
+CHUNK = 512
+LAG = 2
+
+
+def exchange_kernel(
+    chunks, x_ref, g_ref, x_any, g_any, wg_any, wu_any, wd_any,
+    all_x, all_g, terms, back,
+    wg, wu, wd, partial, other, mine, acc,
+    w_sem, y_send, y_recv, x_send, x_recv, c_send, c_recv, f_send, f_recv, own_sem,
+):
+    me = lax.axis_index("outer")
+    across = lax.rem(me + 2, 4)
+    sibling = me + 1 - 2 * lax.rem(me, 2)
+    width = lax.rem(lax.axis_index("dp") + 1, 2)
+    loads = ((wg_any, wg), (wu_any, wu), (wd_any, wd))
+
+    def columns(c):
+        return pl.ds(pl.multiple_of(c * CHUNK, CHUNK), CHUNK)
+
+    def load(c, k):
+        source, target = loads[k]
+        piece = source.at[columns(c), :] if k == 2 else source.at[:, columns(c)]
+        return pltpu.make_async_copy(piece, target.at[c], w_sem.at[k, c])
+
+    def start_loads(c, carry):
+        for k in range(3):
+            load(c, k).start()
+        return carry
+
+    lax.fori_loop(0, chunks, start_loads, 0)
+
+    barrier = pltpu.get_barrier_semaphore()
+    pl.semaphore_signal(barrier, inc=1, device_id={"outer": across}, device_id_type=MESH)
+    pl.semaphore_signal(barrier, inc=1, device_id={"outer": sibling}, device_id_type=MESH)
+    pl.semaphore_signal(barrier, inc=1, device_id={"dp": width}, device_id_type=MESH)
+    pl.semaphore_wait(barrier, 3)
+
+    def remote(source, target, send, recv, axis, peer):
+        return pltpu.make_async_remote_copy(
+            src_ref=source, dst_ref=target, send_sem=send, recv_sem=recv,
+            device_id={axis: peer}, device_id_type=MESH,
+        )
+
+    def act(i):
+        return (x_any, all_x) if i == 0 else (g_any, all_g)
+
+    def act_copies(i):
+        source, target = act(i)
+        place = target.at[me]
+        return (
+            remote(source, place, x_send.at[i], x_recv.at[i], "outer", across),
+            remote(source, place, c_send.at[i], c_recv.at[i], "outer", sibling),
+            pltpu.make_async_copy(source, place, own_sem.at[i]),
+        )
+
+    def term_copies(c):
+        source = mine.at[c]
+        place = terms.at[:, me, :, columns(c)]
+        i = c + 2
+        return (
+            remote(source, place, x_send.at[i], x_recv.at[i], "outer", across),
+            remote(source, place, c_send.at[i], c_recv.at[i], "outer", sibling),
+            pltpu.make_async_copy(source, place, own_sem.at[i]),
+        )
+
+    def act_forward(i):
+        place = act(i)[1].at[across]
+        return remote(place, place, f_send.at[i], f_recv.at[i], "outer", sibling)
+
+    def term_forward(c):
+        place = terms.at[:, across, :, columns(c)]
+        return remote(place, place, f_send.at[c + 2], f_recv.at[c + 2], "outer", sibling)
+
+    def y_copy(c):
+        return remote(partial.at[c], other.at[c], y_send.at[c], y_recv.at[c], "dp", width)
+
+    for i in range(2):
+        for copy in act_copies(i):
+            copy.start()
+    acc[...] = jnp.zeros_like(acc)
+
+    def step(s, carry):
+        @pl.when(s < chunks)
+        def _():
+            for k in range(3):
+                load(s, k).wait()
+            x = x_ref[...]
+            partial[s, 0] = mm(x, wg[s], ((1,), (0,))).astype(BF16)
+            partial[s, 1] = mm(x, wu[s], ((1,), (0,))).astype(BF16)
+            partial[s, 2] = mm(g_ref[...], wd[s], ((1,), (1,))).astype(BF16)
+            y_copy(s).start()
+
+        @pl.when(s >= LAG)
+        def _():
+            c = s - LAG
+            y_copy(c).wait_recv()
+            gate, up, hidden_grad = [
+                partial[c, k].astype(jnp.float32) + other[c, k].astype(jnp.float32) for k in range(3)
+            ]
+            hidden, gate_term, up_term = terms_of(gate, up, hidden_grad)
+            mine[c, 0] = hidden
+            mine[c, 1] = gate_term
+            mine[c, 2] = up_term
+            for copy in term_copies(c):
+                copy.start()
+            acc[...] += mm(gate_term, wg[c], ((1,), (1,))) + mm(up_term, wu[c], ((1,), (1,)))
+
+        return carry
+
+    lax.fori_loop(0, chunks + LAG, step, 0)
+    back[...] = acc[...].astype(BF16)
+
+    for i in range(2):
+        act_copies(i)[0].wait_recv()
+        act_forward(i).start()
+
+    def forward(c, carry):
+        term_copies(c)[0].wait_recv()
+        term_forward(c).start()
+        return carry
+
+    lax.fori_loop(0, chunks, forward, 0)
+
+    def finish(copies, passed):
+        copies[0].wait_send()
+        copies[1].wait()
+        copies[2].wait()
+        passed.wait()
+
+    for i in range(2):
+        finish(act_copies(i), act_forward(i))
+
+    def drain(c, carry):
+        y_copy(c).wait_send()
+        finish(term_copies(c), term_forward(c))
+        return carry
+
+    lax.fori_loop(0, chunks, drain, 0)
+
+
+def exchange(inputs, out_grad, w_gate, w_up, w_down):
+    rows, width = inputs.shape
+    hidden = w_gate.shape[1]
+    chunks = hidden // CHUNK
+    any_spec = pl.BlockSpec(memory_space=pl.ANY)
+    vmem_spec = pl.BlockSpec(memory_space=pltpu.VMEM)
+    dma = pltpu.SemaphoreType.DMA
+    items = dma((chunks + 2,))
+    return pl.pallas_call(
+        functools.partial(exchange_kernel, chunks),
+        out_shape=(
+            jax.ShapeDtypeStruct((4, rows, width), BF16),
+            jax.ShapeDtypeStruct((4, rows, width), BF16),
+            jax.ShapeDtypeStruct((3, 4, rows, hidden), BF16),
+            jax.ShapeDtypeStruct((rows, width), BF16),
+        ),
+        in_specs=[vmem_spec] * 2 + [any_spec] * 5,
+        out_specs=(any_spec, any_spec, any_spec, vmem_spec),
+        scratch_shapes=[
+            pltpu.VMEM((chunks, width, CHUNK), BF16),
+            pltpu.VMEM((chunks, width, CHUNK), BF16),
+            pltpu.VMEM((chunks, CHUNK, width), BF16),
+            pltpu.VMEM((chunks, 3, rows, CHUNK), BF16),
+            pltpu.VMEM((chunks, 3, rows, CHUNK), BF16),
+            pltpu.VMEM((chunks, 3, rows, CHUNK), BF16),
+            pltpu.VMEM((rows, width), jnp.float32),
+            dma((3, chunks)), dma((chunks,)), dma((chunks,)),
+            items, items, items, items, items, items, items,
+        ],
+        compiler_params=pltpu.CompilerParams(
+            collective_id=0, has_side_effects=True, vmem_limit_bytes=56 * 1024 * 1024
+        ),
+    )(inputs, out_grad, inputs, out_grad, w_gate, w_up, w_down)
+
+
+PARTS = 8
+
+
+def grads_kernel(x_ref, g_ref, h_ref, gt_ref, ut_ref, gate_out, up_out, down_out):
+    left = x_ref[...].T
+    for start in range(0, gate_out.shape[1], 1024):
+        cut = slice(start, start + 1024)
+        gate_out[:, cut] = jnp.dot(left, gt_ref[0, :, cut], preferred_element_type=jnp.float32).astype(BF16)
+        up_out[:, cut] = jnp.dot(left, ut_ref[0, :, cut], preferred_element_type=jnp.float32).astype(BF16)
+    left = h_ref[0].T
+    for start in range(0, down_out.shape[1], 1024):
+        cut = slice(start, start + 1024)
+        down_out[:, cut] = jnp.dot(left, g_ref[:, cut], preferred_element_type=jnp.float32).astype(BF16)
+
+
+def weight_grads(all_x, all_g, terms):
+    tokens, width = all_x.shape
+    hidden = terms.shape[2]
+    cost = pl.CostEstimate(
+        flops=6 * tokens * width * hidden,
+        bytes_accessed=2 * (3 * width * hidden + tokens * (2 * width + 3 * hidden)),
+        transcendentals=0,
+    )
+    return pl.pallas_call(
+        grads_kernel,
+        grid=(PARTS,),
+        out_shape=(
+            jax.ShapeDtypeStruct((width, hidden), BF16),
+            jax.ShapeDtypeStruct((width, hidden), BF16),
+            jax.ShapeDtypeStruct((hidden, width), BF16),
+        ),
+        in_specs=[
+            pl.BlockSpec((tokens, width // PARTS), lambda i: (0, i)),
+            pl.BlockSpec((tokens, width), lambda i: (0, 0)),
+            pl.BlockSpec((1, tokens, hidden // PARTS), lambda i: (0, 0, i)),
+            pl.BlockSpec((1, tokens, hidden), lambda i: (1, 0, 0)),
+            pl.BlockSpec((1, tokens, hidden), lambda i: (2, 0, 0)),
+        ],
+        out_specs=(
+            pl.BlockSpec((width // PARTS, hidden), lambda i: (i, 0)),
+            pl.BlockSpec((width // PARTS, hidden), lambda i: (i, 0)),
+            pl.BlockSpec((hidden // PARTS, width), lambda i: (i, 0)),
+        ),
+        compiler_params=pltpu.CompilerParams(vmem_limit_bytes=48 * 1024 * 1024),
+        cost_estimate=cost,
+    )(all_x, all_g, terms, terms, terms)
+
+
+def on_device_kernels(inputs, out_grad, w_gate, w_up, w_down):
+    all_x, all_g, terms, back = exchange(inputs, out_grad, w_gate, w_up, w_down)
+    input_grad = lax.psum(back, "mp")
+    rows, width = inputs.shape
+    hidden = w_gate.shape[1]
+    gate_grad, up_grad, down_grad = weight_grads(
+        all_x.reshape(4 * rows, width), all_g.reshape(4 * rows, width), terms.reshape(3, 4 * rows, hidden)
+    )
+    return input_grad, gate_grad, up_grad, down_grad
+
+
 def solution(mesh):
     dp = mesh.shape["dp"]
     in_specs = (P("outer", "dp"), P("outer", "dp"), P("dp", "mp"), P("dp", "mp"), P("mp", "dp"))
     out_specs = (P("outer", "dp"), P("dp", "mp"), P("dp", "mp"), P("mp", "dp"))
 
     def body(*arrays):
+        rows, width = arrays[0].shape
+        hidden = arrays[2].shape[1]
+        fits = rows % 16 == 0 and 6 * width * hidden <= 40 * 1024 * 1024
+        tiles = width % 1024 == 0 and hidden % 1024 == 0
+        if dp == 2 and mesh.shape["outer"] == 4 and fits and tiles:
+            return on_device_kernels(*arrays)
         return on_device(dp, *arrays)
 
     return jax.shard_map(body, mesh=mesh, in_specs=in_specs, out_specs=out_specs, check_vma=False)

time: 214 us -> 118 us (0.55)
  Pallas kernels: 0 us -> 89.5 us
  waiting for transfers between devices: 85.7 us -> 9.39 us
  matrix products: 69.7 us -> 0 us
  local copies, waits for them, and re-layouts: 36.5 us -> 4.57 us
  starting transfers between devices: 4.1 us -> 0.04 us
    pallas_call x0 -> x2, Pallas kernels: none -> 89.5 us  [the longest x1 64.2 us: exchange(): pl.pallas_call(functools.partial(exchange_kernel, chunks), out_shape=(jax...]
    dot_general x8 -> x0, matrix products: 69.7 us -> none  [mm(): lax.dot_general(left, right, (dims, ((), ())), preferred_element_type=jnp...]
    all_gather x5 -> x0, waiting for transfers between devices: 56.6 us -> none  [the longest x1 26.2 us: on_device(): all_hidden = lax.all_gather(hidden, 'outer', axis=0, tiled=True)]
    unnamed x13 -> x5, local copies, waits for them, and re-layouts: 36.5 us -> 4.57 us
    ppermute x3 -> x0, waiting for transfers between devices: 27.4 us -> none  [summed_over_dp(): other = lax.ppermute(partial, 'dp', [(0, 1), (1, 0)])]
    psum x1, waiting for transfers between devices: 0.01 us -> 9.38 us  [on_device_kernels(): input_grad = lax.psum(back, 'mp')]
    ppermute x3 -> x0, starting transfers between devices: 3.68 us -> none  [summed_over_dp(): other = lax.ppermute(partial, 'dp', [(0, 1), (1, 0)])]
  transfers between devices with their start and end apart: 9 -> 1, of which waited for: 7 -> 1; matrix products, arithmetic and copies ran while one was open for 45% -> 0% of each run, Pallas kernels for 0% -> 22%
where the time goes in v2:
time: 118 us
  Pallas kernels  89.5 us (76%)
  between operations  14 us (12%)
  waiting for transfers between devices  9.39 us (8%)
  local copies, waits for them, and re-layouts  4.57 us (4%)
    pallas_call x1, Pallas kernels, exchange(): pl.pallas_call(functools.partial(exchange_kernel, chunks), out_shape=(jax...  64.2 us
    pallas_call x1, Pallas kernels, weight_grads(): pl.pallas_call(grads_kernel, grid=(PARTS,), out_shape=(jax.ShapeDtypeStru...  25.3 us
    psum x1, waiting for transfers between devices, on_device_kernels(): input_grad = lax.psum(back, 'mp')  9.38 us
    unnamed x5, local copies, waits for them, and re-layouts  4.57 us
  transfers between devices with their start and end apart: 1, of which 1 were waited for; matrix products, arithmetic and copies ran while one was open for 0% of the time, Pallas kernels for 22%

profile of v2, /device:TPU:0, one launch (start us, length us, event | category | flops | bytes accessed | tf_op | source)
XLA Modules:
  0.0 117.6 jit_solution(13791502230121121611)
XLA Ops:
  7.2 0.0 all-reduce.2.cloned.1.call-start
  7.2 64.2 %shard_map.84 = (bf16[4,96,2048]{2,1,0:T(8,128)(2,1)}, bf16[4,96,2048]{2,1,0:T(8,128)(2,1)}, bf16[3,4,96,3072]{3,2,1,0:T(8,128)(2,1)}, bf16[96,2048]{1,0:T(8,128)(2,1)}) custom-call(bf16[96,2048]{1,0:T(8,128)(2,1)} %x_any.1, bf16[96,2048]{1,0:T(8,128)(2,1)} %g_any.1, bf16[96,2048]{1,0:T(8,128)(2,1)} %x_any.1, bf16[96,2048]{1,0:T(8,128)(2,1)} %g_any.1, ...), custom_call_target="tpu_custom_call" | custom-call | tf_op jit(solution)/shard_map/pallas_call | solution.py:208
  71.4 0.0 all-reduce.2.cloned.1.call-update
  71.4 0.0 copy-start
  71.5 1.4 %copy-done = bf16[4,96,2048]{2,1,0:T(8,128)(2,1)S(1)} copy-done((bf16[4,96,2048]{2,1,0:T(8,128)(2,1)S(1)}, bf16[4,96,2048]{2,1,0:T(8,128)(2,1)}, u32[]{:S(2)}) %copy-start) | copy-done | bytes 1572888
  72.9 0.0 copy-start.1
  72.9 1.4 %copy-done.1 = bf16[4,96,2048]{2,1,0:T(8,128)(2,1)S(1)} copy-done((bf16[4,96,2048]{2,1,0:T(8,128)(2,1)S(1)}, bf16[4,96,2048]{2,1,0:T(8,128)(2,1)}, u32[]{:S(2)}) %copy-start.1) | copy-done | bytes 1572888
  74.3 25.3 %shard_map.85 = (bf16[2048,3072]{1,0:T(8,128)(2,1)}, bf16[2048,3072]{1,0:T(8,128)(2,1)}, bf16[3072,2048]{1,0:T(8,128)(2,1)}) custom-call(bf16[384,2048]{1,0:T(8,128)(2,1)S(1)} %bitcast.3, bf16[384,2048]{1,0:T(8,128)(2,1)S(1)} %bitcast.4, bf16[3,384,3072]{2,1,0:T(8,128)(2,1)} %bitcast.5, bf16[3,384,3072]{2,1,0:T(8,128)(2,1)} %bitcast.6, ...), custom_call_target="tpu_custom_call" | custom-call | flops 14495514624 | bytes 47972352 | tf_op jit(solution)/shard_map/pallas_call | solution.py:258
  99.6 9.4 %all-reduce.2.cloned.1.call-done = bf16[96,2048]{1,0:T(8,128)(2,1)} async-done(((bf16[96,2048]{1,0:T(8,128)(2,1)}), bf16[96,2048]{1,0:T(8,128)(2,1)}) %all-reduce.2.cloned.1.call-update) | async-done | bytes 393232 | tf_op jit(solution)/shard_map/psum | solution.py:285
  109.0 1.8 %copy.11 = bf16[96,2048]{1,0:T(8,128)(2,1)} copy(bf16[96,2048]{1,0:T(8,128)(2,1)} %all-reduce.2.cloned.1.call-done) | data formatting | bytes 786432
Async XLA Ops:
  7.2 101.8 %all-reduce.2.cloned.1.call-start = ((), (), s32[]{:S(2)}) async-start(), calls=%async_computation | async-start | bytes 786432 | tf_op jit(solution)/shard_map/psum | solution.py:285
  71.4 1.4 %copy-start = (bf16[4,96,2048]{2,1,0:T(8,128)(2,1)S(1)}, bf16[4,96,2048]{2,1,0:T(8,128)(2,1)}, u32[]{:S(2)}) copy-start(bf16[4,96,2048]{2,1,0:T(8,128)(2,1)} %get-tuple-element.12) | copy-start | bytes 4718596
  72.9 1.4 %copy-start.1 = (bf16[4,96,2048]{2,1,0:T(8,128)(2,1)S(1)}, bf16[4,96,2048]{2,1,0:T(8,128)(2,1)}, u32[]{:S(2)}) copy-start(bf16[4,96,2048]{2,1,0:T(8,128)(2,1)} %get-tuple-element.13) | copy-start | bytes 4718596
Sparse Core Ops, SparseCore 0:
  71.6 37.3 all-reduce.1

commit v3 on v2

--- a/solution.py
+++ b/solution.py
@@ -64,13 +64,22 @@
 def exchange_kernel(
     chunks, x_ref, g_ref, x_any, g_any, wg_any, wu_any, wd_any,
     all_x, all_g, terms, back,
-    wg, wu, wd, partial, other, mine, acc,
+    wg, wu, wd, partial, other, mine, acc, back_out, back_in, back_all,
     w_sem, y_send, y_recv, x_send, x_recv, c_send, c_recv, f_send, f_recv, own_sem,
+    z_send, z_recv, s_send, s_recv, g_send, g_recv,
 ):
     me = lax.axis_index("outer")
     across = lax.rem(me + 2, 4)
     sibling = me + 1 - 2 * lax.rem(me, 2)
     width = lax.rem(lax.axis_index("dp") + 1, 2)
+    level = lax.axis_index("mp")
+    levels = back_all.shape[0]
+    quarter = back_all.shape[2]
+    own_cut = pl.ds(pl.multiple_of(level * quarter, quarter), quarter)
+
+    def above(d):
+        return lax.rem(level + d, levels)
+
     loads = ((wg_any, wg), (wu_any, wu), (wd_any, wd))
 
     def columns(c):
@@ -92,7 +101,9 @@
     pl.semaphore_signal(barrier, inc=1, device_id={"outer": across}, device_id_type=MESH)
     pl.semaphore_signal(barrier, inc=1, device_id={"outer": sibling}, device_id_type=MESH)
     pl.semaphore_signal(barrier, inc=1, device_id={"dp": width}, device_id_type=MESH)
-    pl.semaphore_wait(barrier, 3)
+    for d in range(1, levels):
+        pl.semaphore_signal(barrier, inc=1, device_id={"mp": above(d)}, device_id_type=MESH)
+    pl.semaphore_wait(barrier, 2 + levels)
 
     def remote(source, target, send, recv, axis, peer):
         return pltpu.make_async_remote_copy(
@@ -107,7 +118,10 @@
         source, target = act(i)
         place = target.at[me]
         return (
-            remote(source, place, x_send.at[i], x_recv.at[i], "outer", across),
+            remote(
+                source.at[:, own_cut], target.at[me, :, own_cut],
+                x_send.at[i], x_recv.at[i], "outer", across,
+            ),
             remote(source, place, c_send.at[i], c_recv.at[i], "outer", sibling),
             pltpu.make_async_copy(source, place, own_sem.at[i]),
         )
@@ -122,6 +136,10 @@
             pltpu.make_async_copy(source, place, own_sem.at[i]),
         )
 
+    def act_spread(i, d):
+        place = act(i)[1].at[across, :, own_cut]
+        return remote(place, place, z_send.at[i, d - 1], z_recv.at[i, d - 1], "mp", above(d))
+
     def act_forward(i):
         place = act(i)[1].at[across]
         return remote(place, place, f_send.at[i], f_recv.at[i], "outer", sibling)
@@ -129,6 +147,15 @@
     def term_forward(c):
         place = terms.at[:, across, :, columns(c)]
         return remote(place, place, f_send.at[c + 2], f_recv.at[c + 2], "outer", sibling)
+
+    def back_scatter(d):
+        return remote(
+            back_out.at[above(d)], back_in.at[d - 1], s_send.at[d - 1], s_recv.at[d - 1], "mp", above(d)
+        )
+
+    def back_gather(d):
+        place = back_all.at[level]
+        return remote(place, place, g_send.at[d - 1], g_recv.at[d - 1], "mp", above(d))
 
     def y_copy(c):
         return remote(partial.at[c], other.at[c], y_send.at[c], y_recv.at[c], "dp", width)
@@ -164,13 +191,24 @@
                 copy.start()
             acc[...] += mm(gate_term, wg[c], ((1,), (1,))) + mm(up_term, wu[c], ((1,), (1,)))
 
+        @pl.when(s == 2)
+        def _():
+            for i in range(2):
+                act_copies(i)[0].wait_recv()
+                for d in range(1, levels):
+                    act_spread(i, d).start()
+
         return carry
 
     lax.fori_loop(0, chunks + LAG, step, 0)
-    back[...] = acc[...].astype(BF16)
+    for j in range(levels):
+        back_out[j] = acc[:, j * quarter:(j + 1) * quarter].astype(BF16)
+    for d in range(1, levels):
+        back_scatter(d).start()
 
     for i in range(2):
-        act_copies(i)[0].wait_recv()
+        for d in range(1, levels):
+            act_spread(i, d).wait_recv()
         act_forward(i).start()
 
     def forward(c, carry):
@@ -178,7 +216,25 @@
         term_forward(c).start()
         return carry
 
-    lax.fori_loop(0, chunks, forward, 0)
+    lax.fori_loop(0, chunks - 1, forward, 0)
+
+    total = back_out[level].astype(jnp.float32)
+    for d in range(1, levels):
+        back_scatter(d).wait_recv()
+        total = total + back_in[d - 1].astype(jnp.float32)
+    back_all[level] = total.astype(BF16)
+    for d in range(1, levels):
+        back_gather(d).start()
+
+    forward(chunks - 1, 0)
+
+    for d in range(1, levels):
+        back_gather(d).wait_recv()
+    for j in range(levels):
+        back[:, j * quarter:(j + 1) * quarter] = back_all[j]
+    for d in range(1, levels):
+        back_scatter(d).wait_send()
+        back_gather(d).wait_send()
 
     def finish(copies, passed):
         copies[0].wait_send()
@@ -188,6 +244,8 @@
 
     for i in range(2):
         finish(act_copies(i), act_forward(i))
+        for d in range(1, levels):
+            act_spread(i, d).wait_send()
 
     def drain(c, carry):
         y_copy(c).wait_send()
@@ -197,8 +255,9 @@
     lax.fori_loop(0, chunks, drain, 0)
 
 
-def exchange(inputs, out_grad, w_gate, w_up, w_down):
+def exchange(levels, inputs, out_grad, w_gate, w_up, w_down):
     rows, width = inputs.shape
+    quarter = width // levels
     hidden = w_gate.shape[1]
     chunks = hidden // CHUNK
     any_spec = pl.BlockSpec(memory_space=pl.ANY)
@@ -223,11 +282,16 @@
             pltpu.VMEM((chunks, 3, rows, CHUNK), BF16),
             pltpu.VMEM((chunks, 3, rows, CHUNK), BF16),
             pltpu.VMEM((rows, width), jnp.float32),
+            pltpu.VMEM((levels, rows, quarter), BF16),
+            pltpu.VMEM((levels - 1, rows, quarter), BF16),
+            pltpu.VMEM((levels, rows, quarter), BF16),
             dma((3, chunks)), dma((chunks,)), dma((chunks,)),
             items, items, items, items, items, items, items,
+            dma((2, levels - 1)), dma((2, levels - 1)),
+            dma((levels - 1,)), dma((levels - 1,)), dma((levels - 1,)), dma((levels - 1,)),
         ],
         compiler_params=pltpu.CompilerParams(
-            collective_id=0, has_side_effects=True, vmem_limit_bytes=56 * 1024 * 1024
+            collective_id=0, has_side_effects=True, vmem_limit_bytes=60 * 1024 * 1024
         ),
     )(inputs, out_grad, inputs, out_grad, w_gate, w_up, w_down)
 
@@ -235,7 +299,11 @@
 PARTS = 8
 
 
-def grads_kernel(x_ref, g_ref, h_ref, gt_ref, ut_ref, gate_out, up_out, down_out):
+def grads_kernel(x_ref, g_ref, h_ref, gt_ref, ut_ref, back_ref, gate_out, up_out, down_out, back_out):
+    @pl.when(pl.program_id(0) == 0)
+    def _():
+        back_out[...] = back_ref[...]
+
     left = x_ref[...].T
     for start in range(0, gate_out.shape[1], 1024):
         cut = slice(start, start + 1024)
@@ -247,7 +315,7 @@
         down_out[:, cut] = jnp.dot(left, g_ref[:, cut], preferred_element_type=jnp.float32).astype(BF16)
 
 
-def weight_grads(all_x, all_g, terms):
+def weight_grads(all_x, all_g, terms, back):
     tokens, width = all_x.shape
     hidden = terms.shape[2]
     cost = pl.CostEstimate(
@@ -262,6 +330,7 @@
             jax.ShapeDtypeStruct((width, hidden), BF16),
             jax.ShapeDtypeStruct((width, hidden), BF16),
             jax.ShapeDtypeStruct((hidden, width), BF16),
+            jax.ShapeDtypeStruct(back.shape, BF16),
         ),
         in_specs=[
             pl.BlockSpec((tokens, width // PARTS), lambda i: (0, i)),
@@ -269,24 +338,25 @@
             pl.BlockSpec((1, tokens, hidden // PARTS), lambda i: (0, 0, i)),
             pl.BlockSpec((1, tokens, hidden), lambda i: (1, 0, 0)),
             pl.BlockSpec((1, tokens, hidden), lambda i: (2, 0, 0)),
+            pl.BlockSpec(back.shape, lambda i: (0, 0)),
         ],
         out_specs=(
             pl.BlockSpec((width // PARTS, hidden), lambda i: (i, 0)),
             pl.BlockSpec((width // PARTS, hidden), lambda i: (i, 0)),
             pl.BlockSpec((hidden // PARTS, width), lambda i: (i, 0)),
+            pl.BlockSpec(back.shape, lambda i: (0, 0)),
         ),
-        compiler_params=pltpu.CompilerParams(vmem_limit_bytes=48 * 1024 * 1024),
+        compiler_params=pltpu.CompilerParams(vmem_limit_bytes=60 * 1024 * 1024),
         cost_estimate=cost,
-    )(all_x, all_g, terms, terms, terms)
-
-
-def on_device_kernels(inputs, out_grad, w_gate, w_up, w_down):
-    all_x, all_g, terms, back = exchange(inputs, out_grad, w_gate, w_up, w_down)
-    input_grad = lax.psum(back, "mp")
+    )(all_x, all_g, terms, terms, terms, back)
+
+
+def on_device_kernels(levels, inputs, out_grad, w_gate, w_up, w_down):
+    all_x, all_g, terms, back = exchange(levels, inputs, out_grad, w_gate, w_up, w_down)
     rows, width = inputs.shape
     hidden = w_gate.shape[1]
-    gate_grad, up_grad, down_grad = weight_grads(
-        all_x.reshape(4 * rows, width), all_g.reshape(4 * rows, width), terms.reshape(3, 4 * rows, hidden)
+    gate_grad, up_grad, down_grad, input_grad = weight_grads(
+        all_x.reshape(4 * rows, width), all_g.reshape(4 * rows, width), terms.reshape(3, 4 * rows, hidden), back
     )
     return input_grad, gate_grad, up_grad, down_grad
 
@@ -301,8 +371,8 @@
         hidden = arrays[2].shape[1]
         fits = rows % 16 == 0 and 6 * width * hidden <= 40 * 1024 * 1024
         tiles = width % 1024 == 0 and hidden % 1024 == 0
-        if dp == 2 and mesh.shape["outer"] == 4 and fits and tiles:
-            return on_device_kernels(*arrays)
+        if dp == 2 and mesh.shape["outer"] == 4 and mesh.shape["mp"] == 4 and fits and tiles:
+            return on_device_kernels(mesh.shape["mp"], *arrays)
         return on_device(dp, *arrays)
 
     return jax.shard_map(body, mesh=mesh, in_specs=in_specs, out_specs=out_specs, check_vma=False)

time: 118 us -> 95.5 us (0.81)
  between operations: 14 us -> 0.64 us
  waiting for transfers between devices: 9.39 us -> 0 us
  Pallas kernels: 89.5 us -> 94.7 us
  local copies, waits for them, and re-layouts: 4.57 us -> 0 us
    psum x1 -> x0, waiting for transfers between devices: 9.38 us -> none  [on_device_kernels(): input_grad = lax.psum(back, 'mp')]
    pallas_call x1, Pallas kernels: 64.2 us -> 68.9 us  [exchange(): pl.pallas_call(functools.partial(exchange_kernel, chunks), out_shape=(jax...]
    unnamed x5 -> x0, local copies, waits for them, and re-layouts: 4.57 us -> none
  transfers between devices with their start and end apart: 1 -> 0, of which waited for: 1 -> 0; matrix products, arithmetic and copies ran while one was open for 0% -> 0% of each run, Pallas kernels for 22% -> 0%
where the time goes in v3:
time: 95.5 us; the launch traced here: 95.3 us
  Pallas kernels  94.7 us (99%)
    pallas_call x1, Pallas kernels, exchange(): pl.pallas_call(functools.partial(exchange_kernel, chunks), out_shape=(jax...  68.9 us
    pallas_call x1, Pallas kernels, weight_grads(): pl.pallas_call(grads_kernel, grid=(PARTS,), out_shape=(jax.ShapeDtypeStru...  25.8 us

profile of v3, /device:TPU:0, one launch (start us, length us, event | category | flops | bytes accessed | tf_op | source)
XLA Modules:
  0.0 95.3 jit_solution(12790817048882335448)
XLA Ops:
  0.6 68.9 %shard_map.84 = (bf16[4,96,2048]{2,1,0:T(8,128)(2,1)}, bf16[4,96,2048]{2,1,0:T(8,128)(2,1)}, bf16[3,4,96,3072]{3,2,1,0:T(8,128)(2,1)}, bf16[96,2048]{1,0:T(8,128)(2,1)}) custom-call(bf16[96,2048]{1,0:T(8,128)(2,1)} %x_any.1, bf16[96,2048]{1,0:T(8,128)(2,1)} %g_any.1, bf16[96,2048]{1,0:T(8,128)(2,1)} %x_any.1, bf16[96,2048]{1,0:T(8,128)(2,1)} %g_any.1, ...), custom_call_target="tpu_custom_call" | custom-call | tf_op jit(solution)/shard_map/pallas_call | solution.py:267
  69.6 25.8 %shard_map.85 = (bf16[2048,3072]{1,0:T(8,128)(2,1)}, bf16[2048,3072]{1,0:T(8,128)(2,1)}, bf16[3072,2048]{1,0:T(8,128)(2,1)}, bf16[96,2048]{1,0:T(8,128)(2,1)}) custom-call(bf16[384,2048]{1,0:T(8,128)(2,1)} %bitcast.6, bf16[384,2048]{1,0:T(8,128)(2,1)} %bitcast.7, bf16[3,384,3072]{2,1,0:T(8,128)(2,1)} %bitcast.3, bf16[3,384,3072]{2,1,0:T(8,128)(2,1)} %bitcast.4, ...), custom_call_target="tpu_custom_call" | custom-call | flops 14495514624 | bytes 47972352 | tf_op jit(solution)/shard_map/pallas_call | solution.py:326

commit v4 on v3

--- a/solution.py
+++ b/solution.py
@@ -57,8 +57,9 @@
 
 
 MESH = pl.DeviceIdType.MESH
-CHUNK = 512
+CHUNK = 256
 LAG = 2
+AHEAD = 4
 
 
 def exchange_kernel(
@@ -95,7 +96,7 @@
             load(c, k).start()
         return carry
 
-    lax.fori_loop(0, chunks, start_loads, 0)
+    lax.fori_loop(0, AHEAD, start_loads, 0)
 
     barrier = pltpu.get_barrier_semaphore()
     pl.semaphore_signal(barrier, inc=1, device_id={"outer": across}, device_id_type=MESH)
@@ -175,6 +176,10 @@
             partial[s, 1] = mm(x, wu[s], ((1,), (0,))).astype(BF16)
             partial[s, 2] = mm(g_ref[...], wd[s], ((1,), (1,))).astype(BF16)
             y_copy(s).start()
+
+            @pl.when(s + AHEAD < chunks)
+            def _():
+                start_loads(s + AHEAD, 0)
 
         @pl.when(s >= LAG)
         def _():
@@ -296,7 +301,7 @@
     )(inputs, out_grad, inputs, out_grad, w_gate, w_up, w_down)
 
 
-PARTS = 8
+PARTS = 4
 
 
 def grads_kernel(x_ref, g_ref, h_ref, gt_ref, ut_ref, back_ref, gate_out, up_out, down_out, back_out):

time: 95.5 us -> 93.6 us (0.980)
  Pallas kernels: 94.7 us -> 92.8 us
    pallas_call x1, Pallas kernels: 68.9 us -> 67.3 us  [exchange(): pl.pallas_call(functools.partial(exchange_kernel, chunks), out_shape=(jax...]
where the time goes in v4:
time: 93.6 us; the launch traced here: 93.4 us
  Pallas kernels  92.8 us (99%)
    pallas_call x1, Pallas kernels, exchange(): pl.pallas_call(functools.partial(exchange_kernel, chunks), out_shape=(jax...  67.3 us
    pallas_call x1, Pallas kernels, weight_grads(): pl.pallas_call(grads_kernel, grid=(PARTS,), out_shape=(jax.ShapeDtypeStru...  25.4 us

profile of v4, /device:TPU:0, one launch (start us, length us, event | category | flops | bytes accessed | tf_op | source)
XLA Modules:
  0.0 93.4 jit_solution(6682647127930026965)
XLA Ops:
  0.6 67.3 %shard_map.84 = (bf16[4,96,2048]{2,1,0:T(8,128)(2,1)}, bf16[4,96,2048]{2,1,0:T(8,128)(2,1)}, bf16[3,4,96,3072]{3,2,1,0:T(8,128)(2,1)}, bf16[96,2048]{1,0:T(8,128)(2,1)}) custom-call(bf16[96,2048]{1,0:T(8,128)(2,1)} %x_any.1, bf16[96,2048]{1,0:T(8,128)(2,1)} %g_any.1, bf16[96,2048]{1,0:T(8,128)(2,1)} %x_any.1, bf16[96,2048]{1,0:T(8,128)(2,1)} %g_any.1, ...), custom_call_target="tpu_custom_call" | custom-call | tf_op jit(solution)/shard_map/pallas_call | solution.py:272
  68.0 25.4 %shard_map.85 = (bf16[2048,3072]{1,0:T(8,128)(2,1)}, bf16[2048,3072]{1,0:T(8,128)(2,1)}, bf16[3072,2048]{1,0:T(8,128)(2,1)}, bf16[96,2048]{1,0:T(8,128)(2,1)}) custom-call(bf16[384,2048]{1,0:T(8,128)(2,1)} %bitcast.6, bf16[384,2048]{1,0:T(8,128)(2,1)} %bitcast.7, bf16[3,384,3072]{2,1,0:T(8,128)(2,1)} %bitcast.3, bf16[3,384,3072]{2,1,0:T(8,128)(2,1)} %bitcast.4, ...), custom_call_target="tpu_custom_call" | custom-call | flops 14495514624 | bytes 47972352 | tf_op jit(solution)/shard_map/pallas_call | solution.py:331
